TPU v7x, 32 devices: a whole 2x2x4 slice. The times are simulated.
32 devices in a mesh: qrow: 8 (over y, x, core), dbcol: 4 (over z).
Axes of the slice: x: 2, y: 2, z: 4, core: 2. Of those that a mesh axis runs over, the one named last changes fastest.
Arguments:
- query_desc: bfloat16 [4096, 1024], P('qrow', 'dbcol'), may hold values from -0.1875 to 0.1875
- base_desc: bfloat16 [1024, 1024], P('dbcol', 'qrow'), may hold values from -6 to 6
- slopes: int32 [5], replicated, may hold values from -3 to 3, as said below
Outputs:
- seq_score: bfloat16 [4096, 1024], P('qrow', 'dbcol')
- best_score: float32 [4096], P('qrow')
Inputs may be any that keep to these rules, and one draw needn't show every extreme that they name: `slopes`: 5 distinct values that always include -3 and 3.
All inputs are finite; a program needn't handle non-finite values.
Results may differ from a plain program's by a relative error of at most 0.0041.
Values may be sent and summed in bfloat16 or wider, within the bound.
A program may use at most 64 MiB of HBM per device.

v0:
```python
import math

import jax
import jax.numpy as jnp
from jax import lax
from jax.sharding import PartitionSpec as P

SEQ = 20
WIN = 10
NSLOPE = 5
ROWS_UP = 19
REACH = 57
HALO = 62


spread_floor = 0.5


def passed_along(x, axis, by):
    peers = lax.axis_size(axis)
    pairs = [(i, i + by) for i in range(peers) if 0 <= i + by < peers]
    return lax.ppermute(x, axis, pairs)


def with_halo(cells, sides, width):
    for axis, dim in sides:
        count = lax.axis_size(axis)
        ends = count - 1
        head = lax.slice_in_dim(cells, 0, width, axis=dim)
        tail = lax.slice_in_dim(cells, cells.shape[dim] - width, cells.shape[dim], axis=dim)
        cells = jnp.concatenate(
            [
                lax.ppermute(tail, axis, [(i, (i + 1) % count) for i in range(ends)]),
                cells,
                lax.ppermute(head, axis, [((i + 1) % count, i) for i in range(ends)]),
            ],
            axis=dim,
        )
    return cells


def normalize(similar, valid_cols, valid_rows, out_cols):
    half_win = WIN // 2
    weights = valid_cols.astype(jnp.float32)
    masked = similar * weights[None, :]
    window_sum = masked[:, 0:out_cols]
    window_sq = window_sum * window_sum
    counts = weights[0:out_cols]
    for offset in range(1, WIN):
        column = masked[:, offset : offset + out_cols]
        window_sum = window_sum + column
        window_sq = window_sq + column * column
        counts = counts + weights[offset : offset + out_cols]
    counts = jnp.maximum(counts, 1.0)[None, :]
    window_mean = window_sum / counts
    window_var = window_sq / counts - window_mean * window_mean
    spread = jnp.sqrt(jnp.maximum(window_var, 0.0))
    middle = similar[:, half_win : half_win + out_cols]
    normed = (middle - window_mean) / jnp.maximum(spread, spread_floor)
    keep = (
        weights[half_win : half_win + out_cols][None, :] * valid_rows.astype(jnp.float32)[:, None]
    )
    return (normed * keep).astype(jnp.bfloat16)


def sequence_scores(normed, slopes, tile_rows, tile_cols):
    best_sum = None
    for slope_pos in range(NSLOPE):
        slope_now = slopes[slope_pos]
        running = jnp.zeros((tile_rows, tile_cols), jnp.float32)
        for back_step in range(SEQ):
            row_first = jnp.int32(ROWS_UP - back_step)
            col_first = REACH - slope_now * back_step
            window = lax.dynamic_slice(normed, (row_first, col_first), (tile_rows, tile_cols))
            running = running + window.astype(jnp.float32)
        best_sum = running if best_sum is None else jnp.maximum(best_sum, running)
    return best_sum * (1.0 / math.sqrt(SEQ))


def local(query_desc, base_desc, slopes):
    tile_rows = query_desc.shape[0]
    tile_cols = base_desc.shape[0]
    row_index = lax.axis_index("qrow")
    col_index = lax.axis_index("dbcol")
    total_cols = tile_cols * lax.axis_size("dbcol")
    column_ids = col_index * tile_cols + jnp.arange(tile_cols + 2 * HALO, dtype=jnp.int32) - HALO
    valid_cols = (column_ids >= 0) & (column_ids < total_cols)
    upper_rows = passed_along(query_desc[tile_rows - ROWS_UP :], "qrow", 1)
    query_local = jnp.concatenate([upper_rows, query_desc], 0)
    base_local = with_halo(base_desc, (("dbcol", 0),), HALO)
    query_full = lax.all_gather(query_local, "dbcol", axis=1, tiled=True)
    base_full = lax.all_gather(base_local, "qrow", axis=1, tiled=True)
    similar = lax.dot_general(
        query_full, base_full, (((1,), (1,)), ((), ())), preferred_element_type=jnp.float32
    )
    row_ids = row_index * tile_rows + jnp.arange(tile_rows + ROWS_UP, dtype=jnp.int32) - ROWS_UP
    normed = normalize(similar, valid_cols, row_ids >= 0, tile_cols + 2 * REACH)
    scores = sequence_scores(normed, slopes, tile_rows, tile_cols)
    best_sum = lax.pmax(jnp.max(scores, axis=1), "dbcol")
    return (scores.astype(jnp.bfloat16), best_sum)


def solution(mesh):
    placed = (P("qrow", "dbcol"), P("dbcol", "qrow"), P())
    return jax.shard_map(
        local,
        mesh=mesh,
        in_specs=placed,
        out_specs=(P("qrow", "dbcol"), P("qrow")),
        check_vma=False,
    )
```

profile of v0, /device:TPU:0, one launch (start us, length us, event | category | flops | bytes accessed | tf_op | source)
XLA Modules:
  0.0 149.8 jit_solution(10486370402592812126)
XLA Ops:
  7.2 0.0 all-gather.2.cloned.1.call-start
  7.2 0.7 slice.88
  7.9 0.0 copy-start
  7.9 2.5 %collective-permute-start = (bf16[19,256]{1,0:T(8,128)(2,1)S(1)}, bf16[19,256]{1,0:T(8,128)(2,1)S(1)}, u32[]{:S(2)}, u32[]{:S(2)}) collective-permute-start(bf16[19,256]{1,0:T(8,128)(2,1)S(1)} %slice.88), channel_id=1, source_target_pairs={{0,4},{4,8},{8,12},{12,16},{16,20},{20,24},{24,28},{1,5},{5,9},{9,... | collective-permute-start | bytes 29192 | tf_op jit(solution)/shard_map/ppermute | solution.py:22
  10.4 0.8 collective-permute-done
  11.2 1.7 %pad_maximum_fusion = bf16[531,256]{1,0:T(8,128)(2,1)} fusion(bf16[512,256]{1,0:T(8,128)(2,1)} %param.3, bf16[19,256]{1,0:T(8,128)(2,1)S(1)} %collective-permute-done), kind=kLoop, calls=%fused_computation.105 | loop fusion | flops 543744 | bytes 543744 | tf_op jit(solution)/shard_map/concatenate | solution.py:89
  13.0 0.0 all-gather.2.cloned.1.call-update
  13.0 0.7 fusion.105
  13.7 1.3 collective-permute-start.2
  15.0 4.9 %collective-permute-start.1 = (bf16[62,128]{1,0:T(8,128)(2,1)S(1)}, bf16[62,128]{1,0:T(8,128)(2,1)S(1)}, u32[]{:S(2)}, u32[]{:S(2)}) collective-permute-start(bf16[62,128]{1,0:T(8,128)(2,1)S(1)} %get-tuple-element.4), channel_id=1, source_target_pairs={{0,1},{1,2},{2,3},{4,5},{5,6},{6,7},{8,9},{9,10},{10,11},{12,13},{... | collective-permute-start | bytes 47624 | tf_op jit(solution)/shard_map/ppermute | solution.py:33
  20.0 1.5 %fusion.106 = (s32[1]{0:T(128)}, s32[1]{0:T(128)}, s32[1]{0:T(128)}, s32[1]{0:T(128)}, s32[1]{0:T(128)}) fusion(s32[5]{0:T(128)} %param.5), kind=kLoop, calls=%fused_computation.117 | loop fusion | bytes 40 | tf_op jit(solution)/shard_map/slice | solution.py:69
  86.2 0.1 add_maximum_fusion
  87.1 0.0 collective-permute-done.2
  87.1 0.0 collective-permute-done.1
  87.1 0.0 copy-done
  87.2 14.4 %all_gather.7 = bf16[380,1024]{1,0:T(8,128)(2,1)S(1)} all-gather(bf16[380,128]{1,0:T(8,128)(2,1)S(1)} %pad_maximum_fusion.1), channel_id=1, replica_groups=mesh['qrow'=8,'dbcol'=4] {'qrow'}, dimensions={1}, use_global_device_ids=true | all-gather | bytes 875520 | tf_op jit(solution)/shard_map/all_gather | solution.py:92
  101.5 0.0 all-gather.2.cloned.1.call-done
  101.5 2.0 %broadcast_multiply_fusion = (f32[531,380]{1,0:T(8,128)S(1)}, f32[531,380]{1,0:T(8,128)S(1)}) fusion(f32[380]{0:T(512)S(1)} %fusion.102, bf16[531,1024]{1,0:T(8,128)(2,1)} %all-gather.2.cloned.1.call-done, bf16[380,1024]{1,0:T(8,128)(2,1)S(1)} %all_gather.7), kind=kOutput, calls=%fused_computation.104 | convolution fusion | flops 413447232 | bytes 3481488 | tf_op jit(solution)/shard_map/dot_general | solution.py:93
  103.6 2.3 %fusion.2 = bf16[531,370]{1,0:T(8,128)(2,1)S(1)} fusion(f32[531,380]{1,0:T(8,128)S(1)} %get-tuple-element.13, f32[531,380]{1,0:T(8,128)S(1)} %get-tuple-element.14, f32[531]{0:T(1024)S(1)} %fusion.98, f32[370]{0:T(512)S(1)} %get-tuple-element.7, f32[370]{0:T(512)S(1)} %get-tuple-element.6), kind=kLoop, calls=%fused_computation.8 | loop fusion | flops 7662330 | bytes 9042704 | tf_op jit(solution)/shard_map/convert_element_type | solution.py:63
  105.8 26.6 %fusion.103 = (f32[512]{0:T(512)S(1)}, bf16[512,256]{1,0:T(8,128)(2,1)}) fusion(bf16[531,370]{1,0:T(8,128)(2,1)S(1)} %fusion.2, s32[]{:T(128)S(6)} %select_n.379, s32[]{:T(128)S(6)} %select_n.378, s32[]{:T(128)S(6)} %select_n.377, s32[]{:T(128)S(6)} %select_n.376, s32[]{:T(128)S(6)} %select_n.375, s32[]{:T(128)S(6)} %select_n.374, s32[]{:T(128)S(6)} %select_n.373, ...), kind=kLoop, calls=%fused_computation.115 | loop fusion | flops 25951744 | bytes 25430396 | tf_op jit(solution)/shard_map/reduce_max | solution.py:99
  132.5 10.5 %pmax.7 = f32[512]{0:T(512)} all-reduce(f32[512]{0:T(512)S(1)} %get-tuple-element.2), channel_id=1, replica_groups=mesh['qrow'=8,'dbcol'=4] {'dbcol'}, use_global_device_ids=true, to_apply=%region_1.0 | all-reduce | flops 512 | bytes 4096 | tf_op jit(solution)/shard_map/pmax | solution.py:99
  (3 shorter events, 0.0 us)
Async XLA Ops:
  7.2 94.4 %all-gather.2.cloned.1.call-start = ((), (), s32[]{:S(2)}) async-start(), calls=%async_computation | async-start | bytes 1372160 | tf_op jit(solution)/shard_map/all_gather | solution.py:91
  7.9 79.2 %copy-start = (bf16[256,128]{1,0:T(8,128)(2,1)S(1)}, bf16[256,128]{1,0:T(8,128)(2,1)}, u32[]{:S(2)}) copy-start(bf16[256,128]{1,0:T(8,128)(2,1)} %param.4) | copy-start | bytes 196612
  7.9 3.3 %collective-permute-start = (bf16[19,256]{1,0:T(8,128)(2,1)S(1)}, bf16[19,256]{1,0:T(8,128)(2,1)S(1)}, u32[]{:S(2)}, u32[]{:S(2)}) collective-permute-start(bf16[19,256]{1,0:T(8,128)(2,1)S(1)} %slice.88), channel_id=1, source_target_pairs={{0,4},{4,8},{8,12},{12,16},{16,20},{20,24},{24,28},{1,5},{5,9},{9,... | collective-permute-start | bytes 29192 | tf_op jit(solution)/shard_map/ppermute | solution.py:22
  13.7 73.4 %collective-permute-start.2 = (bf16[62,128]{1,0:T(8,128)(2,1)S(1)}, bf16[62,128]{1,0:T(8,128)(2,1)S(1)}, u32[]{:S(2)}, u32[]{:S(2)}) collective-permute-start(bf16[62,128]{1,0:T(8,128)(2,1)S(1)} %get-tuple-element.5), channel_id=1, source_target_pairs={{1,0},{2,1},{3,2},{5,4},{6,5},{7,6},{9,8},{10,9},{11,10},{13,12},{... | collective-permute-start | bytes 47624 | tf_op jit(solution)/shard_map/ppermute | solution.py:35
  15.0 72.1 %collective-permute-start.1 = (bf16[62,128]{1,0:T(8,128)(2,1)S(1)}, bf16[62,128]{1,0:T(8,128)(2,1)S(1)}, u32[]{:S(2)}, u32[]{:S(2)}) collective-permute-start(bf16[62,128]{1,0:T(8,128)(2,1)S(1)} %get-tuple-element.4), channel_id=1, source_target_pairs={{0,1},{1,2},{2,3},{4,5},{5,6},{6,7},{8,9},{9,10},{10,11},{12,13},{... | collective-permute-start | bytes 47624 | tf_op jit(solution)/shard_map/ppermute | solution.py:33
Sparse Core Ops, SparseCore 0:
  13.1 35.3 all-gather.1
where the time goes:
time: 151 us; the launch traced here: 150 us
  between operations  79.6 us (53%)
  other arithmetic  30.8 us (20%)
  blocking collectives  24.9 us (16%)
  starting transfers between devices  8.73 us (6%)
  local copies, waits for them, and re-layouts  2.98 us (2%)
  matrix products  2 us (1%)
    reduce_max x1, other arithmetic, local(): best_sum = lax.pmax(jnp.max(scores, axis=1), 'dbcol')  26.6 us
    all_gather x1, blocking collectives, local(): base_full = lax.all_gather(base_local, 'qrow', axis=1, tiled=True)  14.4 us
    pmax x1, blocking collectives, local(): best_sum = lax.pmax(jnp.max(scores, axis=1), 'dbcol')  10.5 us
    ppermute x1, starting transfers between devices, with_halo(): lax.ppermute(tail, axis, [(i, (i + 1) % count) for i in range(ends)])  4.94 us
  transfers between devices with their start and end apart: 4, of which 1 were waited for; matrix products, arithmetic and copies ran while one was open for 2% of the time, Pallas kernels for 0%

commit v1 on v0

v1 whole, which is shorter than its diff:
```python
import functools
import math

import jax
import jax.numpy as jnp
from jax import lax
from jax.experimental import pallas as pl
from jax.experimental.pallas import tpu as pltpu
from jax.sharding import PartitionSpec as P

SEQ = 20
WIN = 10
SMAX = 3
NSLOPE = 5

SPREAD_FLOOR = 0.5
SIDE = 64
ABOVE = 24
EARLY = 32
STEP = 128
SUB, LANE = 8, 128
MESH = pl.DeviceIdType.MESH


def rolled(x, by):
    by %= x.shape[1]
    return pltpu.roll(x, by, 1) if by else x


def sheared(x, by, slope):
    if not slope:
        return rolled(x, by)
    width, tiles = x.shape[1], []
    for r in range(0, x.shape[0], SUB):
        tile, shift = x[r : r + SUB, :], (by + slope * r) % width
        if shift % LANE + slope * (SUB - 1) <= LANE:
            tile = pltpu.roll(tile, shift, 1, stride=slope, stride_axis=0)
        else:
            tile = rolled(pltpu.roll(tile, 0, 1, stride=slope, stride_axis=0), shift)
        tiles.append(tile)
    return jnp.concatenate(tiles, 0)


def window_sum(x):
    two = x + rolled(x, -1)
    four = two + rolled(two, -2)
    eight = four + rolled(four, -4)
    return rolled(eight + rolled(two, -8), WIN // 2)


def kernel(
    nq, nz, q_ref, b_ref, slopes_ref, seq_ref, best_ref, qs, bs, normed, tops,
    own_sem, side_send, side_recv, base_send, base_recv, ring_send, ring_recv,
    query_send, query_recv, up_send, up_recv, top_send, top_recv,
):
    me_q, me_z = lax.axis_index("qrow"), lax.axis_index("dbcol")
    rows, depth = q_ref.shape
    cols, base_depth = b_ref.shape
    width = cols + 2 * SIDE
    total = cols * nz
    first, last = me_z == 0, me_z == nz - 1

    def remote(src, dst, send, recv, q, z):
        return pltpu.make_async_remote_copy(
            src_ref=src, dst_ref=dst, send_sem=send, recv_sem=recv,
            device_id=(q, z), device_id_type=MESH,
        )

    slot_depth = bs.shape[2]

    def mine(start, count):
        if slot_depth == base_depth:
            return me_q, pl.ds(start, count), pl.ds(0, base_depth)
        return 0, pl.ds(start, count), pl.ds(pl.multiple_of(me_q * base_depth, LANE), base_depth)

    own = [
        pltpu.make_async_copy(q_ref, qs.at[me_z], own_sem.at[0]),
        pltpu.make_async_copy(b_ref, bs.at[mine(0, cols)], own_sem.at[1]),
    ]
    for copy in own:
        copy.start()

    q_peers = [lax.rem(me_q + d, nq) for d in range(1, nq)]
    z_peers = [lax.rem(me_z + d, nz) for d in range(1, nz)]
    barrier = pltpu.get_barrier_semaphore()
    for z in z_peers:
        pl.semaphore_signal(barrier, inc=1, device_id=(me_q, z), device_id_type=MESH)
    for q in q_peers:
        pl.semaphore_signal(barrier, inc=1, device_id=(q, me_z), device_id_type=MESH)

    @pl.when(last)
    def _():
        bs[mine(cols, SIDE)] = jnp.zeros((SIDE, base_depth), bs.dtype)

    @pl.when(first)
    def _():
        bs[mine(cols + SIDE, SIDE)] = jnp.zeros((SIDE, base_depth), bs.dtype)

    @pl.when(me_q == 0)
    def _():
        normed[0:ABOVE, :] = jnp.zeros((ABOVE, width), normed.dtype)

    pl.semaphore_wait(barrier, nq + nz - 2)

    to_left = remote(
        b_ref.at[pl.ds(0, SIDE), :], bs.at[mine(cols, SIDE)],
        side_send.at[0], side_recv.at[0], me_q, lax.max(me_z - 1, 0),
    )
    to_right = remote(
        b_ref.at[pl.ds(cols - SIDE, SIDE), :], bs.at[mine(cols + SIDE, SIDE)],
        side_send.at[1], side_recv.at[1], me_q, lax.min(me_z + 1, nz - 1),
    )

    @pl.when(jnp.logical_not(first))
    def _():
        to_left.start()

    @pl.when(jnp.logical_not(last))
    def _():
        to_right.start()

    pieces = [(rows - EARLY, EARLY)]
    pieces += [(r, min(STEP, rows - EARLY - r)) for r in range(0, rows, STEP)]

    def send_query(p):
        start, count = pieces[p]
        copies = [
            remote(
                q_ref.at[pl.ds(start, count), :], qs.at[me_z, pl.ds(start, count), :],
                query_send.at[p, d], query_recv.at[p, d], me_q, z,
            )
            for d, z in enumerate(z_peers)
        ]
        for copy in copies:
            copy.start()
        return copies

    query = [send_query(0)]
    base = [
        remote(b_ref, bs.at[mine(0, cols)], base_send.at[d], base_recv.at[d], q, me_z)
        for d, q in enumerate(q_peers)
    ]
    for copy in base:
        copy.start()
    for p in range(1, len(pieces)):
        query.append(send_query(p))

    @pl.when(jnp.logical_not(last))
    def _():
        to_left.wait_recv()

    @pl.when(jnp.logical_not(first))
    def _():
        to_right.wait_recv()

    sides = bs.at[mine(cols, 2 * SIDE)]
    ring = [
        remote(sides, sides, ring_send.at[d], ring_recv.at[d], q, me_z)
        for d, q in enumerate(q_peers)
    ]
    for copy in ring:
        copy.start()
    for copy in own:
        copy.wait()
    for copy in base + ring:
        copy.wait_recv()

    place = lax.broadcasted_iota(jnp.int32, (1, width), 1)
    frame = me_z * cols + jnp.where(place < cols + SIDE, place, place - width)
    inside = (frame >= 0) & (frame < total)
    reach = jnp.minimum(frame + WIN // 2, total) - jnp.maximum(frame - WIN // 2, 0)
    share = 1.0 / jnp.maximum(reach, 1).astype(jnp.float32)

    def normalize(start, count):
        similar = None
        deep = min(depth, slot_depth)
        for f in range(0, depth * nz, deep):
            part = lax.dot_general(
                qs[f // depth, start : start + count, f % depth : f % depth + deep],
                bs[f // slot_depth, :, f % slot_depth : f % slot_depth + deep],
                (((1,), (1,)), ((), ())), preferred_element_type=jnp.float32,
            )
            similar = part if similar is None else similar + part
        mean = window_sum(similar) * share
        var = window_sum(similar * similar) * share - mean * mean
        value = (similar - mean) * lax.rsqrt(jnp.maximum(var, SPREAD_FLOOR * SPREAD_FLOOR))
        value = jnp.where(inside, value, 0.0)
        normed[ABOVE + start : ABOVE + start + count, :] = value.astype(jnp.bfloat16).astype(
            jnp.float32
        )

    tried = {}
    for v in range(-SMAX, SMAX + 1):
        used = slopes_ref[0] == v
        for a in range(1, NSLOPE):
            used = used | (slopes_ref[a] == v)
        tried[v] = jnp.where(used, 0.0, -jnp.inf)

    span = ABOVE + STEP
    out_row = lax.broadcasted_iota(jnp.int32, (STEP, span), 0) + ABOVE
    in_row = lax.broadcasted_iota(jnp.int32, (STEP, span), 1)

    def summing(out, into):
        return ((into <= out) & (into > out - SEQ)).astype(jnp.bfloat16)

    band = summing(out_row, in_row)
    band_turned_in = summing(out_row, span - 1 - in_row)
    band_turned_out = summing(span + ABOVE - 1 - out_row, in_row)

    def turning(n, kind):
        row = lax.broadcasted_iota(jnp.int32, (n, n), 0)
        return (row + lax.broadcasted_iota(jnp.int32, (n, n), 1) == n - 1).astype(kind)

    turn_in, turn_out = turning(span, jnp.bfloat16), turning(STEP, jnp.float32)

    def score(start):
        block = normed[start : start + span, :]
        exact = block.astype(jnp.bfloat16)
        best = jnp.dot(band, exact, preferred_element_type=jnp.float32)[:, :cols] + tried[0]
        turned = jnp.dot(turn_in, exact, preferred_element_type=jnp.float32)
        down = None
        for v in range(1, SMAX + 1):
            lined = sheared(turned, -v * (span - 1), v).astype(jnp.bfloat16)
            sums = jnp.dot(band_turned_in, lined, preferred_element_type=jnp.float32)
            sums = sheared(sums, v * ABOVE, v)[:, :cols]
            best = jnp.maximum(best, sums + tried[v])
            lined = sheared(block, 0, v).astype(jnp.bfloat16)
            sums = jnp.dot(band_turned_out, lined, preferred_element_type=jnp.float32)
            sums = sheared(sums, -v * (span - 1), v)[:, :cols]
            sums = sums if v == SMAX else sums + tried[-v]
            down = sums if down is None else jnp.maximum(down, sums)
        down = jnp.dot(
            turn_out, down, precision=lax.Precision.HIGHEST, preferred_element_type=jnp.float32
        )
        best = jnp.maximum(best, down)
        best = best * (1.0 / math.sqrt(SEQ))
        seq_ref[start : start + STEP, :] = best.astype(seq_ref.dtype)
        top = best[:, 0:128]
        for c in range(128, cols, 128):
            top = jnp.maximum(top, best[:, c : c + 128])
        n = start // STEP
        tops[0, n : n + 1, :] = jnp.max(top.T, axis=0, keepdims=True)

    for copy in query[0]:
        copy.wait_recv()
    normalize(*pieces[0])
    up = remote(
        normed.at[pl.ds(rows, ABOVE), :], normed.at[pl.ds(0, ABOVE), :],
        up_send, up_recv, lax.min(me_q + 1, nq - 1), me_z,
    )

    @pl.when(me_q < nq - 1)
    def _():
        up.start()

    for p in range(1, len(pieces)):
        for copy in query[p]:
            copy.wait_recv()
        normalize(*pieces[p])
        if p == 1:

            @pl.when(me_q > 0)
            def _():
                up.wait_recv()

        score(pieces[p][0])

    peaks = [
        remote(tops.at[0], tops.at[1 + d], top_send.at[d], top_recv.at[d], me_q, z)
        for d, z in enumerate(z_peers)
    ]
    for copy in peaks:
        copy.start()

    @pl.when(jnp.logical_not(first))
    def _():
        to_left.wait_send()

    @pl.when(jnp.logical_not(last))
    def _():
        to_right.wait_send()

    @pl.when(me_q < nq - 1)
    def _():
        up.wait_send()

    for copy in base + ring:
        copy.wait_send()
    for copies in query:
        for copy in copies:
            copy.wait_send()
    for copy in peaks:
        copy.wait()
    best = tops[0]
    for d in range(1, nz):
        best = jnp.maximum(best, tops[d])
    best_ref[...] = best


def solution(mesh):
    nq, nz = mesh.shape["qrow"], mesh.shape["dbcol"]

    def local(query_desc, base_desc, slopes):
        rows, depth = query_desc.shape
        cols, base_depth = base_desc.shape
        width = cols + 2 * SIDE
        slots = (nq, width, base_depth) if base_depth % LANE else (1, width, base_depth * nq)
        steps = rows // STEP
        dma = pltpu.SemaphoreType.DMA
        any_space = pl.BlockSpec(memory_space=pl.ANY)
        vmem = pl.BlockSpec(memory_space=pltpu.VMEM)
        seq_score, best = pl.pallas_call(
            functools.partial(kernel, nq, nz),
            out_shape=(
                jax.ShapeDtypeStruct((rows, cols), jnp.bfloat16),
                jax.ShapeDtypeStruct((steps, STEP), jnp.float32),
            ),
            in_specs=[any_space, any_space, pl.BlockSpec(memory_space=pltpu.SMEM)],
            out_specs=(vmem, vmem),
            scratch_shapes=[
                pltpu.VMEM((nz, rows, depth), jnp.bfloat16),
                pltpu.VMEM(slots, jnp.bfloat16),
                pltpu.VMEM((ABOVE + rows, width), jnp.float32),
                pltpu.VMEM((nz, steps, STEP), jnp.float32),
                dma((2,)),
                dma((2,)),
                dma((2,)),
                dma((nq - 1,)),
                dma((nq - 1,)),
                dma((nq - 1,)),
                dma((nq - 1,)),
                dma((steps + 1, nz - 1)),
                dma((steps + 1, nz - 1)),
                dma(()),
                dma(()),
                dma((nz - 1,)),
                dma((nz - 1,)),
            ],
            compiler_params=pltpu.CompilerParams(
                collective_id=0, has_side_effects=True, vmem_limit_bytes=40 << 20
            ),
            cost_estimate=pl.CostEstimate(
                flops=2 * rows * width * depth * nz,
                bytes_accessed=4 * rows * cols,
                transcendentals=rows * width,
            ),
        )(query_desc, base_desc, slopes)
        return seq_score, best.reshape(rows)

    return jax.shard_map(
        local,
        mesh=mesh,
        in_specs=(P("qrow", "dbcol"), P("dbcol", "qrow"), P()),
        out_specs=(P("qrow", "dbcol"), P("qrow")),
        check_vma=False,
    )
```

time: 151 us -> 42.2 us (0.28)
  between operations: 79.6 us -> 0.65 us
  Pallas kernels: 0 us -> 37.7 us
  other arithmetic: 30.8 us -> 0 us
  blocking collectives: 24.9 us -> 0 us
  starting transfers between devices: 8.73 us -> 0 us
  matrix products: 2 us -> 0 us
    pallas_call x0 -> x1, Pallas kernels: none -> 37.7 us  [local(): pl.pallas_call(functools.partial(kernel, nq, nz), out_shape=(jax.ShapeDty...]
    reduce_max x1 -> x0, other arithmetic: 26.6 us -> none  [local(): best_sum = lax.pmax(jnp.max(scores, axis=1), 'dbcol')]
    all_gather x1 -> x0, blocking collectives: 14.4 us -> none  [local(): base_full = lax.all_gather(base_local, 'qrow', axis=1, tiled=True)]
    pmax x1 -> x0, blocking collectives: 10.5 us -> none  [local(): best_sum = lax.pmax(jnp.max(scores, axis=1), 'dbcol')]
    ppermute x3 -> x0, starting transfers between devices: 8.7 us -> none  [the longest x1 4.94 us: with_halo(): lax.ppermute(tail, axis, [(i, (i + 1) % count) for i in range(ends)])]
    unnamed x2 -> x8, local copies, waits for them, and re-layouts: 0.01 us -> 3.72 us
    slice x3 -> x0, local copies, waits for them, and re-layouts: 2.97 us -> none  [the longest x1 1.51 us: sequence_scores(): slope_now = slopes[slope_pos]]
    convert_element_type x3 -> x0, other arithmetic: 2.3 us -> none  [the longest x1 2.28 us: normalize(): return (normed * keep).astype(jnp.bfloat16)]
  transfers between devices with their start and end apart: 4 -> 0, of which waited for: 1 -> 0; matrix products, arithmetic and copies ran while one was open for 2% -> 0% of each run, Pallas kernels for 0% -> 0%
where the time goes in v1:
time: 42.2 us; the launch traced here: 42 us
  Pallas kernels  37.7 us (89%)
  local copies, waits for them, and re-layouts  3.72 us (9%)
  between operations  0.65 us (2%)
    pallas_call x1, Pallas kernels, local(): pl.pallas_call(functools.partial(kernel, nq, nz), out_shape=(jax.ShapeDty...  37.7 us
    unnamed x8, local copies, waits for them, and re-layouts  3.72 us

profile of v1, /device:TPU:0, one launch (start us, length us, event | category | flops | bytes accessed | tf_op | source)
XLA Modules:
  0.0 42.0 jit_solution(15794685644278968859)
XLA Ops:
  0.6 0.0 copy-start
  0.6 0.9 %copy-done = bf16[512,256]{1,0:T(8,128)(2,1)S(1)} copy-done((bf16[512,256]{1,0:T(8,128)(2,1)S(1)}, bf16[512,256]{1,0:T(8,128)(2,1)}, u32[]{:S(2)}) %copy-start) | copy-done | bytes 262168
  1.6 0.0 copy-start.1
  1.6 0.8 %copy-done.1 = bf16[256,128]{1,0:T(8,128)(2,1)S(1)} copy-done((bf16[256,128]{1,0:T(8,128)(2,1)S(1)}, bf16[256,128]{1,0:T(8,128)(2,1)}, u32[]{:S(2)}) %copy-start.1) | copy-done | bytes 65560
  2.4 0.0 copy-start.2
  2.4 0.7 %copy-done.2 = s32[5]{0:T(128)S(1)} copy-done((s32[5]{0:T(128)S(1)}, s32[5]{0:T(128)}, u32[]{:S(2)}) %copy-start.2) | copy-done | bytes 44
  3.1 37.7 %shard_map.50 = (bf16[512,256]{1,0:T(8,128)(2,1)S(1)}, f32[4,128]{1,0:T(4,128)S(1)}) custom-call(bf16[512,256]{1,0:T(8,128)(2,1)S(1)} %copy-done, bf16[256,128]{1,0:T(8,128)(2,1)S(1)} %copy-done.1, s32[5]{0:T(128)S(1)} %copy-done.2), custom_call_target="tpu_custom_call" | custom-call | flops 402653184 | bytes 524288 | tf_op jit(solution)/shard_map/pallas_call | solution.py:312
  40.8 0.7 %copy.7 = bf16[512,256]{1,0:T(8,128)(2,1)} copy(bf16[512,256]{1,0:T(8,128)(2,1)S(1)} %get-tuple-element.8) | data formatting | bytes 524288
  41.5 0.6 %copy.8 = f32[512]{0:T(512)} copy(f32[512]{0:T(512)S(1)} %bitcast.1) | data formatting | bytes 4096
Async XLA Ops:
  0.6 1.0 %copy-start = (bf16[512,256]{1,0:T(8,128)(2,1)S(1)}, bf16[512,256]{1,0:T(8,128)(2,1)}, u32[]{:S(2)}) copy-start(bf16[512,256]{1,0:T(8,128)(2,1)} %q_ref.1) | copy-start | bytes 786436
  1.6 0.8 %copy-start.1 = (bf16[256,128]{1,0:T(8,128)(2,1)S(1)}, bf16[256,128]{1,0:T(8,128)(2,1)}, u32[]{:S(2)}) copy-start(bf16[256,128]{1,0:T(8,128)(2,1)} %b_ref.1) | copy-start | bytes 196612
  2.4 0.7 %copy-start.2 = (s32[5]{0:T(128)S(1)}, s32[5]{0:T(128)}, u32[]{:S(2)}) copy-start(s32[5]{0:T(128)} %slopes_ref.1) | copy-start | bytes 64

commit v2 on v1

--- a/solution.py
+++ b/solution.py
@@ -17,6 +17,7 @@
 SIDE = 64
 ABOVE = 24
 EARLY = 32
+AHEAD = 3
 STEP = 128
 SUB, LANE = 8, 128
 MESH = pl.DeviceIdType.MESH
@@ -49,8 +50,8 @@
 
 
 def kernel(
-    nq, nz, q_ref, b_ref, slopes_ref, seq_ref, best_ref, qs, bs, normed, tops,
-    own_sem, side_send, side_recv, base_send, base_recv, ring_send, ring_recv,
+    nq, nz, q_ref, b_ref, slopes_hbm, seq_hbm, best_ref, seq_ref, qs, bs, bt, normed, tops, slopes_ref,
+    own_sem, out_sem, side_send, side_recv, base_send, base_recv, ring_send, ring_recv,
     query_send, query_recv, up_send, up_recv, top_send, top_recv,
 ):
     me_q, me_z = lax.axis_index("qrow"), lax.axis_index("dbcol")
@@ -76,6 +77,7 @@
     own = [
         pltpu.make_async_copy(q_ref, qs.at[me_z], own_sem.at[0]),
         pltpu.make_async_copy(b_ref, bs.at[mine(0, cols)], own_sem.at[1]),
+        pltpu.make_async_copy(slopes_hbm, slopes_ref, own_sem.at[2]),
     ]
     for copy in own:
         copy.start()
@@ -142,7 +144,7 @@
     ]
     for copy in base:
         copy.start()
-    for p in range(1, len(pieces)):
+    for p in range(1, AHEAD):
         query.append(send_query(p))
 
     @pl.when(jnp.logical_not(last))
@@ -162,8 +164,17 @@
         copy.start()
     for copy in own:
         copy.wait()
-    for copy in base + ring:
-        copy.wait_recv()
+    for d in range(nq):
+        q = lax.rem(me_q + nq - d, nq)
+        if d:
+            base[d - 1].wait_recv()
+            ring[d - 1].wait_recv()
+        start = pl.multiple_of(q * base_depth, base_depth)
+        if slot_depth == base_depth:
+            part = bs[q, :, :]
+        else:
+            part = bs[0, :, pl.ds(start, base_depth)]
+        bt[pl.ds(start, base_depth), :] = part.T
 
     place = lax.broadcasted_iota(jnp.int32, (1, width), 1)
     frame = me_z * cols + jnp.where(place < cols + SIDE, place, place - width)
@@ -173,12 +184,10 @@
 
     def normalize(start, count):
         similar = None
-        deep = min(depth, slot_depth)
-        for f in range(0, depth * nz, deep):
-            part = lax.dot_general(
-                qs[f // depth, start : start + count, f % depth : f % depth + deep],
-                bs[f // slot_depth, :, f % slot_depth : f % slot_depth + deep],
-                (((1,), (1,)), ((), ())), preferred_element_type=jnp.float32,
+        for z in range(nz):
+            part = jnp.dot(
+                qs[z, start : start + count, :], bt[z * depth : (z + 1) * depth, :],
+                preferred_element_type=jnp.float32,
             )
             similar = part if similar is None else similar + part
         mean = window_sum(similar) * share
@@ -212,6 +221,8 @@
         return (row + lax.broadcasted_iota(jnp.int32, (n, n), 1) == n - 1).astype(kind)
 
     turn_in, turn_out = turning(span, jnp.bfloat16), turning(STEP, jnp.float32)
+
+    written = []
 
     def score(start):
         block = normed[start : start + span, :]
@@ -234,7 +245,14 @@
         )
         best = jnp.maximum(best, down)
         best = best * (1.0 / math.sqrt(SEQ))
-        seq_ref[start : start + STEP, :] = best.astype(seq_ref.dtype)
+        done = pl.ds(start, STEP)
+        seq_ref[done, :] = best.astype(seq_ref.dtype)
+        written.append(
+            pltpu.make_async_copy(
+                seq_ref.at[done, :], seq_hbm.at[done, :], out_sem.at[start // STEP]
+            )
+        )
+        written[-1].start()
         top = best[:, 0:128]
         for c in range(128, cols, 128):
             top = jnp.maximum(top, best[:, c : c + 128])
@@ -256,6 +274,10 @@
     for p in range(1, len(pieces)):
         for copy in query[p]:
             copy.wait_recv()
+        if p + AHEAD - 1 < len(pieces):
+            for copy in query[p]:
+                copy.wait_send()
+            query.append(send_query(p + AHEAD - 1))
         normalize(*pieces[p])
         if p == 1:
 
@@ -286,10 +308,10 @@
 
     for copy in base + ring:
         copy.wait_send()
-    for copies in query:
-        for copy in copies:
+    for p in [0] + list(range(max(1, len(pieces) - AHEAD + 1), len(pieces))):
+        for copy in query[p]:
             copy.wait_send()
-    for copy in peaks:
+    for copy in written + peaks:
         copy.wait()
     best = tops[0]
     for d in range(1, nz):
@@ -307,7 +329,7 @@
         slots = (nq, width, base_depth) if base_depth % LANE else (1, width, base_depth * nq)
         steps = rows // STEP
         dma = pltpu.SemaphoreType.DMA
-        any_space = pl.BlockSpec(memory_space=pl.ANY)
+        hbm = pl.BlockSpec(memory_space=pltpu.HBM)
         vmem = pl.BlockSpec(memory_space=pltpu.VMEM)
         seq_score, best = pl.pallas_call(
             functools.partial(kernel, nq, nz),
@@ -315,14 +337,18 @@
                 jax.ShapeDtypeStruct((rows, cols), jnp.bfloat16),
                 jax.ShapeDtypeStruct((steps, STEP), jnp.float32),
             ),
-            in_specs=[any_space, any_space, pl.BlockSpec(memory_space=pltpu.SMEM)],
-            out_specs=(vmem, vmem),
+            in_specs=[hbm, hbm, hbm],
+            out_specs=(hbm, vmem),
             scratch_shapes=[
+                pltpu.VMEM((rows, cols), jnp.bfloat16),
                 pltpu.VMEM((nz, rows, depth), jnp.bfloat16),
                 pltpu.VMEM(slots, jnp.bfloat16),
+                pltpu.VMEM((base_depth * nq, width), jnp.bfloat16),
                 pltpu.VMEM((ABOVE + rows, width), jnp.float32),
                 pltpu.VMEM((nz, steps, STEP), jnp.float32),
-                dma((2,)),
+                pltpu.SMEM((NSLOPE,), jnp.int32),
+                dma((3,)),
+                dma((steps,)),
                 dma((2,)),
                 dma((2,)),
                 dma((nq - 1,)),
@@ -337,7 +363,7 @@
                 dma((nz - 1,)),
             ],
             compiler_params=pltpu.CompilerParams(
-                collective_id=0, has_side_effects=True, vmem_limit_bytes=40 << 20
+                collective_id=0, has_side_effects=True, vmem_limit_bytes=60 << 20
             ),
             cost_estimate=pl.CostEstimate(
                 flops=2 * rows * width * depth * nz,

time: 42.2 us -> 41 us (0.972)
  local copies, waits for them, and re-layouts: 3.72 us -> 2.25 us
    unnamed x8 -> x4, local copies, waits for them, and re-layouts: 3.72 us -> 2.25 us
where the time goes in v2:
time: 41 us; the launch traced here: 40.8 us
  Pallas kernels  37.9 us (92%)
  local copies, waits for them, and re-layouts  2.25 us (5%)
  between operations  0.65 us (2%)
    pallas_call x1, Pallas kernels, local(): pl.pallas_call(functools.partial(kernel, nq, nz), out_shape=(jax.ShapeDty...  37.9 us
    unnamed x4, local copies, waits for them, and re-layouts  2.25 us

profile of v2, /device:TPU:0, one launch (start us, length us, event | category | flops | bytes accessed | tf_op | source)
XLA Modules:
  0.0 40.8 jit_solution(4029823271267983215)
XLA Ops:
  0.6 37.9 %shard_map.50 = (bf16[512,256]{1,0:T(8,128)(2,1)}, f32[4,128]{1,0:T(4,128)}) custom-call(bf16[512,256]{1,0:T(8,128)(2,1)} %q_ref.1, bf16[256,128]{1,0:T(8,128)(2,1)} %b_ref.1, s32[5]{0:T(128)} %slopes_hbm.1), custom_call_target="tpu_custom_call" | custom-call | flops 402653184 | bytes 524288 | tf_op jit(solution)/shard_map/pallas_call | solution.py:334
  38.5 0.0 copy-start
  38.6 1.7 %copy.7 = bf16[512,256]{1,0:T(8,128)(2,1)} copy(bf16[512,256]{1,0:T(8,128)(2,1)} %get-tuple-element.8) | data formatting | bytes 524288
  40.2 0.0 copy-done
  40.2 0.6 %copy.8 = f32[512]{0:T(512)} copy(f32[512]{0:T(512)S(1)} %bitcast.1) | data formatting | bytes 4096
Async XLA Ops:
  38.5 1.7 %copy-start = (f32[4,128]{1,0:T(4,128)S(1)}, f32[4,128]{1,0:T(4,128)}, u32[]{:S(2)}) copy-start(f32[4,128]{1,0:T(4,128)} %get-tuple-element.5) | copy-start | bytes 6148

commit v3 on v2

--- a/solution.py
+++ b/solution.py
@@ -51,7 +51,7 @@
 
 def kernel(
     nq, nz, q_ref, b_ref, slopes_hbm, seq_hbm, best_ref, seq_ref, qs, bs, bt, normed, tops, slopes_ref,
-    own_sem, out_sem, side_send, side_recv, base_send, base_recv, ring_send, ring_recv,
+    own_sem, out_sem, side_send, side_recv, base_send, base_recv, pass_send, pass_recv,
     query_send, query_recv, up_send, up_recv, top_send, top_recv,
 ):
     me_q, me_z = lax.axis_index("qrow"), lax.axis_index("dbcol")
@@ -137,44 +137,55 @@
             copy.start()
         return copies
 
-    query = [send_query(0)]
+    query = [send_query(p) for p in range(AHEAD - 1)]
+
+    @pl.when(jnp.logical_not(last))
+    def _():
+        to_left.wait_recv()
+
+    @pl.when(jnp.logical_not(first))
+    def _():
+        to_right.wait_recv()
+
+    for copy in own:
+        copy.wait()
+
+    def block(q):
+        if slot_depth == base_depth:
+            return bs.at[q]
+        start = pl.multiple_of(q * base_depth, LANE)
+        return bs.at[0, :, pl.ds(start, base_depth)]
+
+    def hand_on(q, d):
+        copy = remote(block(q), block(q), pass_send.at[d], pass_recv.at[d], mate, me_z)
+        copy.start()
+        return copy
+
+    def turn(q):
+        start = pl.multiple_of(q * base_depth, base_depth)
+        bt[pl.ds(start, base_depth), :] = block(q)[...].T
+
+    mate = me_q + 1 - 2 * lax.rem(me_q, 2)
     base = [
-        remote(b_ref, bs.at[mine(0, cols)], base_send.at[d], base_recv.at[d], q, me_z)
-        for d, q in enumerate(q_peers)
+        remote(
+            block(me_q), block(me_q), base_send.at[d - 1], base_recv.at[d - 1],
+            lax.rem(me_q + 2 * d, nq), me_z,
+        )
+        for d in range(1, nq // 2)
     ]
     for copy in base:
         copy.start()
-    for p in range(1, AHEAD):
-        query.append(send_query(p))
-
-    @pl.when(jnp.logical_not(last))
-    def _():
-        to_left.wait_recv()
-
-    @pl.when(jnp.logical_not(first))
-    def _():
-        to_right.wait_recv()
-
-    sides = bs.at[mine(cols, 2 * SIDE)]
-    ring = [
-        remote(sides, sides, ring_send.at[d], ring_recv.at[d], q, me_z)
-        for d, q in enumerate(q_peers)
-    ]
-    for copy in ring:
-        copy.start()
-    for copy in own:
-        copy.wait()
-    for d in range(nq):
-        q = lax.rem(me_q + nq - d, nq)
-        if d:
-            base[d - 1].wait_recv()
-            ring[d - 1].wait_recv()
-        start = pl.multiple_of(q * base_depth, base_depth)
-        if slot_depth == base_depth:
-            part = bs[q, :, :]
-        else:
-            part = bs[0, :, pl.ds(start, base_depth)]
-        bt[pl.ds(start, base_depth), :] = part.T
+    handed = [hand_on(me_q, 0)]
+    query.append(send_query(AHEAD - 1))
+    turn(me_q)
+    for d in range(1, nq // 2):
+        base[d - 1].wait_recv()
+        q = lax.rem(me_q + nq - 2 * d, nq)
+        handed.append(hand_on(q, d))
+        turn(q)
+    for d in range(nq // 2):
+        handed[d].wait_recv()
+        turn(lax.rem(mate + nq - 2 * d, nq))
 
     place = lax.broadcasted_iota(jnp.int32, (1, width), 1)
     frame = me_z * cols + jnp.where(place < cols + SIDE, place, place - width)
@@ -306,7 +317,7 @@
     def _():
         up.wait_send()
 
-    for copy in base + ring:
+    for copy in base + handed:
         copy.wait_send()
     for p in [0] + list(range(max(1, len(pieces) - AHEAD + 1), len(pieces))):
         for copy in query[p]:
@@ -351,10 +362,10 @@
                 dma((steps,)),
                 dma((2,)),
                 dma((2,)),
-                dma((nq - 1,)),
-                dma((nq - 1,)),
-                dma((nq - 1,)),
-                dma((nq - 1,)),
+                dma((nq // 2 - 1,)),
+                dma((nq // 2 - 1,)),
+                dma((nq // 2,)),
+                dma((nq // 2,)),
                 dma((steps + 1, nz - 1)),
                 dma((steps + 1, nz - 1)),
                 dma(()),

time: 41 us -> 40.4 us (0.985)
  Pallas kernels: 37.9 us -> 37.3 us
    pallas_call x1, Pallas kernels: 37.9 us -> 37.3 us  [local(): pl.pallas_call(functools.partial(kernel, nq, nz), out_shape=(jax.ShapeDty...]
where the time goes in v3:
time: 40.4 us; the launch traced here: 40.2 us
  Pallas kernels  37.3 us (92%)
  local copies, waits for them, and re-layouts  2.25 us (6%)
  between operations  0.65 us (2%)
    pallas_call x1, Pallas kernels, local(): pl.pallas_call(functools.partial(kernel, nq, nz), out_shape=(jax.ShapeDty...  37.3 us
    unnamed x4, local copies, waits for them, and re-layouts  2.25 us

profile of v3, /device:TPU:0, one launch (start us, length us, event | category | flops | bytes accessed | tf_op | source)
XLA Modules:
  0.0 40.2 jit_solution(3766334600418497457)
XLA Ops:
  0.6 37.3 %shard_map.50 = (bf16[512,256]{1,0:T(8,128)(2,1)}, f32[4,128]{1,0:T(4,128)}) custom-call(bf16[512,256]{1,0:T(8,128)(2,1)} %q_ref.1, bf16[256,128]{1,0:T(8,128)(2,1)} %b_ref.1, s32[5]{0:T(128)} %slopes_hbm.1), custom_call_target="tpu_custom_call" | custom-call | flops 402653184 | bytes 524288 | tf_op jit(solution)/shard_map/pallas_call | solution.py:345
  38.0 0.0 copy-start
  38.0 1.7 %copy.7 = bf16[512,256]{1,0:T(8,128)(2,1)} copy(bf16[512,256]{1,0:T(8,128)(2,1)} %get-tuple-element.8) | data formatting | bytes 524288
  39.7 0.0 copy-done
  39.7 0.6 %copy.8 = f32[512]{0:T(512)} copy(f32[512]{0:T(512)S(1)} %bitcast.1) | data formatting | bytes 4096
Async XLA Ops:
  38.0 1.7 %copy-start = (f32[4,128]{1,0:T(4,128)S(1)}, f32[4,128]{1,0:T(4,128)}, u32[]{:S(2)}) copy-start(f32[4,128]{1,0:T(4,128)} %get-tuple-element.5) | copy-start | bytes 6148

commit v4 on v2

--- a/solution.py
+++ b/solution.py
@@ -17,7 +17,6 @@
 SIDE = 64
 ABOVE = 24
 EARLY = 32
-AHEAD = 3
 STEP = 128
 SUB, LANE = 8, 128
 MESH = pl.DeviceIdType.MESH
@@ -50,9 +49,10 @@
 
 
 def kernel(
-    nq, nz, q_ref, b_ref, slopes_hbm, seq_hbm, best_ref, seq_ref, qs, bs, bt, normed, tops, slopes_ref,
-    own_sem, out_sem, side_send, side_recv, base_send, base_recv, ring_send, ring_recv,
-    query_send, query_recv, up_send, up_recv, top_send, top_recv,
+    nq, nz, q_ref, b_ref, slopes_hbm, seq_hbm, best_ref, seq_ref, qs, bs, bt, normed, made, given,
+    tops, slopes_ref,
+    own_sem, out_sem, side_send, side_recv, base_send, base_recv, pass_send, pass_recv,
+    query_send, query_recv, given_send, given_recv, up_send, up_recv, top_send, top_recv,
 ):
     me_q, me_z = lax.axis_index("qrow"), lax.axis_index("dbcol")
     rows, depth = q_ref.shape
@@ -67,16 +67,22 @@
             device_id=(q, z), device_id_type=MESH,
         )
 
-    slot_depth = bs.shape[2]
-
-    def mine(start, count):
+    slot_depth = bs.shape[3]
+
+    inner = jnp.logical_not(first | last)
+    beside_first, beside_last = me_z == 1, me_z == nz - 2
+    beside = beside_first | beside_last
+    end = jnp.where(me_z <= 1, 0, nz - 1)
+
+    def block(k, q, start=0, count=width):
         if slot_depth == base_depth:
-            return me_q, pl.ds(start, count), pl.ds(0, base_depth)
-        return 0, pl.ds(start, count), pl.ds(pl.multiple_of(me_q * base_depth, LANE), base_depth)
+            return bs.at[k, q, pl.ds(start, count), :]
+        at = pl.multiple_of(q * base_depth, LANE)
+        return bs.at[k, 0, pl.ds(start, count), pl.ds(at, base_depth)]
 
     own = [
         pltpu.make_async_copy(q_ref, qs.at[me_z], own_sem.at[0]),
-        pltpu.make_async_copy(b_ref, bs.at[mine(0, cols)], own_sem.at[1]),
+        pltpu.make_async_copy(b_ref, block(0, me_q, 0, cols), own_sem.at[1]),
         pltpu.make_async_copy(slopes_hbm, slopes_ref, own_sem.at[2]),
     ]
     for copy in own:
@@ -90,14 +96,6 @@
     for q in q_peers:
         pl.semaphore_signal(barrier, inc=1, device_id=(q, me_z), device_id_type=MESH)
 
-    @pl.when(last)
-    def _():
-        bs[mine(cols, SIDE)] = jnp.zeros((SIDE, base_depth), bs.dtype)
-
-    @pl.when(first)
-    def _():
-        bs[mine(cols + SIDE, SIDE)] = jnp.zeros((SIDE, base_depth), bs.dtype)
-
     @pl.when(me_q == 0)
     def _():
         normed[0:ABOVE, :] = jnp.zeros((ABOVE, width), normed.dtype)
@@ -105,88 +103,152 @@
     pl.semaphore_wait(barrier, nq + nz - 2)
 
     to_left = remote(
-        b_ref.at[pl.ds(0, SIDE), :], bs.at[mine(cols, SIDE)],
+        b_ref.at[pl.ds(0, SIDE), :], block(0, me_q, cols, SIDE),
         side_send.at[0], side_recv.at[0], me_q, lax.max(me_z - 1, 0),
     )
     to_right = remote(
-        b_ref.at[pl.ds(cols - SIDE, SIDE), :], bs.at[mine(cols + SIDE, SIDE)],
+        b_ref.at[pl.ds(cols - SIDE, SIDE), :], block(0, me_q, cols + SIDE, SIDE),
         side_send.at[1], side_recv.at[1], me_q, lax.min(me_z + 1, nz - 1),
     )
-
-    @pl.when(jnp.logical_not(first))
+    from_end = remote(
+        b_ref, block(1, me_q, 0, cols), side_send.at[2], side_recv.at[2],
+        me_q, jnp.where(first, 1, nz - 2),
+    )
+    sends_left, sends_right = (me_z >= 2) & (me_z <= nz - 2), (me_z >= 1) & (me_z <= nz - 3)
+
+    @pl.when(sends_left)
     def _():
         to_left.start()
 
-    @pl.when(jnp.logical_not(last))
+    @pl.when(sends_right)
     def _():
         to_right.start()
+
+    @pl.when(first | last)
+    def _():
+        from_end.start()
 
     pieces = [(rows - EARLY, EARLY)]
     pieces += [(r, min(STEP, rows - EARLY - r)) for r in range(0, rows, STEP)]
 
+    def query_copy(p, z):
+        start, count = pieces[p]
+        return remote(
+            q_ref.at[pl.ds(start, count), :], qs.at[me_z, pl.ds(start, count), :],
+            query_send.at[p, z - 1], query_recv.at[p, me_z], me_q, z,
+        )
+
     def send_query(p):
+        for z in range(1, nz - 1):
+
+            @pl.when(me_z != z)
+            def _():
+                query_copy(p, z).start()
+
+    def wait_query(p):
         start, count = pieces[p]
-        copies = [
-            remote(
-                q_ref.at[pl.ds(start, count), :], qs.at[me_z, pl.ds(start, count), :],
-                query_send.at[p, d], query_recv.at[p, d], me_q, z,
-            )
-            for d, z in enumerate(z_peers)
-        ]
-        for copy in copies:
-            copy.start()
-        return copies
-
-    query = [send_query(0)]
-    base = [
-        remote(b_ref, bs.at[mine(0, cols)], base_send.at[d], base_recv.at[d], q, me_z)
-        for d, q in enumerate(q_peers)
-    ]
-    for copy in base:
-        copy.start()
-    for p in range(1, AHEAD):
-        query.append(send_query(p))
-
-    @pl.when(jnp.logical_not(last))
-    def _():
-        to_left.wait_recv()
-
-    @pl.when(jnp.logical_not(first))
-    def _():
-        to_right.wait_recv()
-
-    sides = bs.at[mine(cols, 2 * SIDE)]
-    ring = [
-        remote(sides, sides, ring_send.at[d], ring_recv.at[d], q, me_z)
-        for d, q in enumerate(q_peers)
-    ]
-    for copy in ring:
-        copy.start()
+        for z in range(nz):
+
+            @pl.when(me_z != z)
+            def _():
+                remote(
+                    q_ref.at[pl.ds(start, count), :], qs.at[z, pl.ds(start, count), :],
+                    query_send.at[p, 0], query_recv.at[p, z], me_q, z,
+                ).wait_recv()
+
+    for p in range(2):
+        send_query(p)
+
     for copy in own:
         copy.wait()
-    for d in range(nq):
-        q = lax.rem(me_q + nq - d, nq)
-        if d:
-            base[d - 1].wait_recv()
-            ring[d - 1].wait_recv()
+
+    @pl.when(sends_right)
+    def _():
+        to_left.wait_recv()
+
+    @pl.when(sends_left)
+    def _():
+        to_right.wait_recv()
+
+    @pl.when(beside)
+    def _():
+        from_end.wait_recv()
+
+    nothing = jnp.zeros((SIDE, base_depth), bs.dtype)
+
+    @pl.when(beside_first)
+    def _():
+        block(0, me_q, cols + SIDE, SIDE)[...] = block(1, me_q, cols - SIDE, SIDE)[...]
+        block(1, me_q, cols, SIDE)[...] = block(0, me_q, 0, SIDE)[...]
+        block(1, me_q, cols + SIDE, SIDE)[...] = nothing
+
+    @pl.when(beside_last)
+    def _():
+        block(0, me_q, cols, SIDE)[...] = block(1, me_q, 0, SIDE)[...]
+        block(1, me_q, cols + SIDE, SIDE)[...] = block(0, me_q, cols - SIDE, SIDE)[...]
+        block(1, me_q, cols, SIDE)[...] = nothing
+
+    mate = me_q + 1 - 2 * lax.rem(me_q, 2)
+
+    def hand_on(k, q, d):
+        return remote(block(k, q), block(k, q), pass_send.at[k, d], pass_recv.at[k, d], mate, me_z)
+
+    def turn(k, q):
         start = pl.multiple_of(q * base_depth, base_depth)
-        if slot_depth == base_depth:
-            part = bs[q, :, :]
-        else:
-            part = bs[0, :, pl.ds(start, base_depth)]
-        bt[pl.ds(start, base_depth), :] = part.T
+        bt[k, pl.ds(start, base_depth), :] = block(k, q)[...].T
+
+    def base_copy(k, d):
+        return remote(
+            block(k, me_q), block(k, me_q), base_send.at[k, d - 1], base_recv.at[k, d - 1],
+            lax.rem(me_q + 2 * d, nq), me_z,
+        )
+
+    sets = [(1, beside), (0, inner)]
+    for k, takes in sets:
+
+        @pl.when(takes)
+        def _():
+            for d in range(1, nq // 2):
+                base_copy(k, d).start()
+            hand_on(k, me_q, 0).start()
+
+    for p in range(2, len(pieces)):
+        send_query(p)
+
+    for k, takes in sets:
+
+        @pl.when(takes)
+        def _():
+            turn(k, me_q)
+            for d in range(1, nq // 2):
+                base_copy(k, d).wait_recv()
+                q = lax.rem(me_q + nq - 2 * d, nq)
+                hand_on(k, q, d).start()
+                turn(k, q)
+
+    for k, takes in sets:
+
+        @pl.when(takes)
+        def _():
+            for d in range(nq // 2):
+                q = lax.rem(mate + nq - 2 * d, nq)
+                hand_on(k, q, d).wait_recv()
+                turn(k, q)
 
     place = lax.broadcasted_iota(jnp.int32, (1, width), 1)
-    frame = me_z * cols + jnp.where(place < cols + SIDE, place, place - width)
-    inside = (frame >= 0) & (frame < total)
-    reach = jnp.minimum(frame + WIN // 2, total) - jnp.maximum(frame - WIN // 2, 0)
-    share = 1.0 / jnp.maximum(reach, 1).astype(jnp.float32)
-
-    def normalize(start, count):
+
+    def around(z):
+        frame = z * cols + jnp.where(place < cols + SIDE, place, place - width)
+        reach = jnp.minimum(frame + WIN // 2, total) - jnp.maximum(frame - WIN // 2, 0)
+        share = 1.0 / jnp.maximum(reach, 1).astype(jnp.float32)
+        return (frame >= 0) & (frame < total), share
+
+    def normalize(k, start, count):
+        inside, share = around(end if k else me_z)
         similar = None
         for z in range(nz):
             part = jnp.dot(
-                qs[z, start : start + count, :], bt[z * depth : (z + 1) * depth, :],
+                qs[z, start : start + count, :], bt[k, z * depth : (z + 1) * depth, :],
                 preferred_element_type=jnp.float32,
             )
             similar = part if similar is None else similar + part
@@ -194,9 +256,36 @@
         var = window_sum(similar * similar) * share - mean * mean
         value = (similar - mean) * lax.rsqrt(jnp.maximum(var, SPREAD_FLOOR * SPREAD_FLOOR))
         value = jnp.where(inside, value, 0.0)
-        normed[ABOVE + start : ABOVE + start + count, :] = value.astype(jnp.bfloat16).astype(
-            jnp.float32
-        )
+        return value.astype(jnp.bfloat16)
+
+    def give(p):
+        rows_now = pl.ds(*pieces[p])
+        return remote(
+            made.at[rows_now, :], given.at[rows_now, :], given_send.at[p], given_recv.at[p],
+            me_q, end,
+        )
+
+    def normalize_part(p):
+        start, count = pieces[p]
+        own_rows = pl.ds(ABOVE + start, count)
+
+        @pl.when(inner)
+        def _():
+            wait_query(p)
+
+        @pl.when(beside)
+        def _():
+            made[pl.ds(start, count), :] = normalize(1, start, count)
+            give(p).start()
+
+        @pl.when(inner)
+        def _():
+            normed[own_rows, :] = normalize(0, start, count).astype(jnp.float32)
+
+        @pl.when(first | last)
+        def _():
+            give(p).wait_recv()
+            normed[own_rows, :] = given[pl.ds(start, count), :].astype(jnp.float32)
 
     tried = {}
     for v in range(-SMAX, SMAX + 1):
@@ -259,9 +348,7 @@
         n = start // STEP
         tops[0, n : n + 1, :] = jnp.max(top.T, axis=0, keepdims=True)
 
-    for copy in query[0]:
-        copy.wait_recv()
-    normalize(*pieces[0])
+    normalize_part(0)
     up = remote(
         normed.at[pl.ds(rows, ABOVE), :], normed.at[pl.ds(0, ABOVE), :],
         up_send, up_recv, lax.min(me_q + 1, nq - 1), me_z,
@@ -272,13 +359,7 @@
         up.start()
 
     for p in range(1, len(pieces)):
-        for copy in query[p]:
-            copy.wait_recv()
-        if p + AHEAD - 1 < len(pieces):
-            for copy in query[p]:
-                copy.wait_send()
-            query.append(send_query(p + AHEAD - 1))
-        normalize(*pieces[p])
+        normalize_part(p)
         if p == 1:
 
             @pl.when(me_q > 0)
@@ -294,23 +375,43 @@
     for copy in peaks:
         copy.start()
 
-    @pl.when(jnp.logical_not(first))
+    @pl.when(sends_left)
     def _():
         to_left.wait_send()
 
-    @pl.when(jnp.logical_not(last))
+    @pl.when(sends_right)
     def _():
         to_right.wait_send()
 
+    @pl.when(first | last)
+    def _():
+        from_end.wait_send()
+
+    for k, takes in sets:
+
+        @pl.when(takes)
+        def _():
+            for d in range(1, nq // 2):
+                base_copy(k, d).wait_send()
+            for d in range(nq // 2):
+                hand_on(k, lax.rem(me_q + nq - 2 * d, nq), d).wait_send()
+
+    for p in range(len(pieces)):
+
+        @pl.when(beside)
+        def _():
+            give(p).wait_send()
+
+        for z in range(1, nz - 1):
+
+            @pl.when(me_z != z)
+            def _():
+                query_copy(p, z).wait_send()
+
     @pl.when(me_q < nq - 1)
     def _():
         up.wait_send()
 
-    for copy in base + ring:
-        copy.wait_send()
-    for p in [0] + list(range(max(1, len(pieces) - AHEAD + 1), len(pieces))):
-        for copy in query[p]:
-            copy.wait_send()
     for copy in written + peaks:
         copy.wait()
     best = tops[0]
@@ -342,21 +443,25 @@
             scratch_shapes=[
                 pltpu.VMEM((rows, cols), jnp.bfloat16),
                 pltpu.VMEM((nz, rows, depth), jnp.bfloat16),
-                pltpu.VMEM(slots, jnp.bfloat16),
-                pltpu.VMEM((base_depth * nq, width), jnp.bfloat16),
+                pltpu.VMEM((2, *slots), jnp.bfloat16),
+                pltpu.VMEM((2, base_depth * nq, width), jnp.bfloat16),
                 pltpu.VMEM((ABOVE + rows, width), jnp.float32),
+                pltpu.VMEM((rows, width), jnp.bfloat16),
+                pltpu.VMEM((rows, width), jnp.bfloat16),
                 pltpu.VMEM((nz, steps, STEP), jnp.float32),
                 pltpu.SMEM((NSLOPE,), jnp.int32),
                 dma((3,)),
                 dma((steps,)),
-                dma((2,)),
-                dma((2,)),
-                dma((nq - 1,)),
-                dma((nq - 1,)),
-                dma((nq - 1,)),
-                dma((nq - 1,)),
-                dma((steps + 1, nz - 1)),
-                dma((steps + 1, nz - 1)),
+                dma((3,)),
+                dma((3,)),
+                dma((2, nq // 2 - 1)),
+                dma((2, nq // 2 - 1)),
+                dma((2, nq // 2)),
+                dma((2, nq // 2)),
+                dma((steps + 1, nz - 2)),
+                dma((steps + 1, nz)),
+                dma((steps + 1,)),
+                dma((steps + 1,)),
                 dma(()),
                 dma(()),
                 dma((nz - 1,)),

time: 41 us -> 44 us (1.073)
  Pallas kernels: 37.9 us -> 41 us
    pallas_call x1, Pallas kernels: 37.9 us -> 41 us  [local(): pl.pallas_call(functools.partial(kernel, nq, nz), out_shape=(jax.ShapeDty...]
where the time goes in v4:
time: 44 us; the launch traced here: 43.9 us
  Pallas kernels  41 us (93%)
  local copies, waits for them, and re-layouts  2.25 us (5%)
  between operations  0.65 us (1%)
    pallas_call x1, Pallas kernels, local(): pl.pallas_call(functools.partial(kernel, nq, nz), out_shape=(jax.ShapeDty...  41 us
    unnamed x4, local copies, waits for them, and re-layouts  2.25 us

profile of v4, /device:TPU:0, one launch (start us, length us, event | category | flops | bytes accessed | tf_op | source)
XLA Modules:
  0.0 43.9 jit_solution(15150256357109588357)
XLA Ops:
  0.6 41.0 %shard_map.50 = (bf16[512,256]{1,0:T(8,128)(2,1)}, f32[4,128]{1,0:T(4,128)}) custom-call(bf16[512,256]{1,0:T(8,128)(2,1)} %q_ref.1, bf16[256,128]{1,0:T(8,128)(2,1)} %b_ref.1, s32[5]{0:T(128)} %slopes_hbm.1), custom_call_target="tpu_custom_call" | custom-call | flops 402653184 | bytes 524288 | tf_op jit(solution)/shard_map/pallas_call | solution.py:435
  41.6 0.0 copy-start
  41.6 1.7 %copy.7 = bf16[512,256]{1,0:T(8,128)(2,1)} copy(bf16[512,256]{1,0:T(8,128)(2,1)} %get-tuple-element.8) | data formatting | bytes 524288
  43.3 0.0 copy-done
  43.3 0.6 %copy.8 = f32[512]{0:T(512)} copy(f32[512]{0:T(512)S(1)} %bitcast.1) | data formatting | bytes 4096
Async XLA Ops:
  41.6 1.7 %copy-start = (f32[4,128]{1,0:T(4,128)S(1)}, f32[4,128]{1,0:T(4,128)}, u32[]{:S(2)}) copy-start(f32[4,128]{1,0:T(4,128)} %get-tuple-element.5) | copy-start | bytes 6148

commit v5 on v3

--- a/solution.py
+++ b/solution.py
@@ -231,7 +231,7 @@
         row = lax.broadcasted_iota(jnp.int32, (n, n), 0)
         return (row + lax.broadcasted_iota(jnp.int32, (n, n), 1) == n - 1).astype(kind)
 
-    turn_in, turn_out = turning(span, jnp.bfloat16), turning(STEP, jnp.float32)
+    turn_in, turn_out = turning(span, jnp.bfloat16), turning(STEP, jnp.bfloat16)
 
     written = []
 
@@ -240,20 +240,33 @@
         exact = block.astype(jnp.bfloat16)
         best = jnp.dot(band, exact, preferred_element_type=jnp.float32)[:, :cols] + tried[0]
         turned = jnp.dot(turn_in, exact, preferred_element_type=jnp.float32)
+        slopes = range(1, SMAX + 1)
+        lined = [sheared(turned, -v * (span - 1), v).astype(jnp.bfloat16) for v in slopes]
+        ups = jnp.dot(
+            band_turned_in, jnp.concatenate(lined, 1), preferred_element_type=jnp.float32
+        )
+        lined = [sheared(block, 0, v).astype(jnp.bfloat16) for v in slopes]
+        downs = jnp.dot(
+            band_turned_out, jnp.concatenate(lined, 1), preferred_element_type=jnp.float32
+        )
         down = None
-        for v in range(1, SMAX + 1):
-            lined = sheared(turned, -v * (span - 1), v).astype(jnp.bfloat16)
-            sums = jnp.dot(band_turned_in, lined, preferred_element_type=jnp.float32)
-            sums = sheared(sums, v * ABOVE, v)[:, :cols]
-            best = jnp.maximum(best, sums + tried[v])
-            lined = sheared(block, 0, v).astype(jnp.bfloat16)
-            sums = jnp.dot(band_turned_out, lined, preferred_element_type=jnp.float32)
-            sums = sheared(sums, -v * (span - 1), v)[:, :cols]
+        for v in slopes:
+            at = (v - 1) * width
+            sums = sheared(downs[:, at : at + width], -v * (span - 1), v)[:, :cols]
             sums = sums if v == SMAX else sums + tried[-v]
             down = sums if down is None else jnp.maximum(down, sums)
-        down = jnp.dot(
-            turn_out, down, precision=lax.Precision.HIGHEST, preferred_element_type=jnp.float32
-        )
+        high = down.astype(jnp.bfloat16)
+        rest = down - high.astype(jnp.float32)
+        middle = rest.astype(jnp.bfloat16)
+        low = (rest - middle.astype(jnp.float32)).astype(jnp.bfloat16)
+        parts = jnp.dot(
+            turn_out, jnp.concatenate([high, middle, low], 1), preferred_element_type=jnp.float32
+        )
+        for v in slopes:
+            at = (v - 1) * width
+            sums = sheared(ups[:, at : at + width], v * ABOVE, v)[:, :cols]
+            best = jnp.maximum(best, sums + tried[v])
+        down = parts[:, :cols] + (parts[:, cols : 2 * cols] + parts[:, 2 * cols :])
         best = jnp.maximum(best, down)
         best = best * (1.0 / math.sqrt(SEQ))
         done = pl.ds(start, STEP)

time: 40.4 us -> 40.2 us (level)
  no operation moved by 1% of the time
where the time goes in v5:
time: 40.2 us; the launch traced here: 40 us
  Pallas kernels  37.1 us (92%)
  local copies, waits for them, and re-layouts  2.25 us (6%)
  between operations  0.65 us (2%)
    pallas_call x1, Pallas kernels, local(): pl.pallas_call(functools.partial(kernel, nq, nz), out_shape=(jax.ShapeDty...  37.1 us
    unnamed x4, local copies, waits for them, and re-layouts  2.25 us

profile of v5, /device:TPU:0, one launch (start us, length us, event | category | flops | bytes accessed | tf_op | source)
XLA Modules:
  0.0 40.0 jit_solution(5047546080472362906)
XLA Ops:
  0.6 37.1 %shard_map.50 = (bf16[512,256]{1,0:T(8,128)(2,1)}, f32[4,128]{1,0:T(4,128)}) custom-call(bf16[512,256]{1,0:T(8,128)(2,1)} %q_ref.1, bf16[256,128]{1,0:T(8,128)(2,1)} %b_ref.1, s32[5]{0:T(128)} %slopes_hbm.1), custom_call_target="tpu_custom_call" | custom-call | flops 402653184 | bytes 524288 | tf_op jit(solution)/shard_map/pallas_call | solution.py:358
  37.8 0.0 copy-start
  37.8 1.7 %copy.7 = bf16[512,256]{1,0:T(8,128)(2,1)} copy(bf16[512,256]{1,0:T(8,128)(2,1)} %get-tuple-element.8) | data formatting | bytes 524288
  39.5 0.0 copy-done
  39.5 0.6 %copy.8 = f32[512]{0:T(512)} copy(f32[512]{0:T(512)S(1)} %bitcast.1) | data formatting | bytes 4096
Async XLA Ops:
  37.8 1.7 %copy-start = (f32[4,128]{1,0:T(4,128)S(1)}, f32[4,128]{1,0:T(4,128)}, u32[]{:S(2)}) copy-start(f32[4,128]{1,0:T(4,128)} %get-tuple-element.5) | copy-start | bytes 6148

commit v6 on v5

--- a/solution.py
+++ b/solution.py
@@ -17,7 +17,6 @@
 SIDE = 64
 ABOVE = 24
 EARLY = 32
-AHEAD = 3
 STEP = 128
 SUB, LANE = 8, 128
 MESH = pl.DeviceIdType.MESH
@@ -122,7 +121,8 @@
         to_right.start()
 
     pieces = [(rows - EARLY, EARLY)]
-    pieces += [(r, min(STEP, rows - EARLY - r)) for r in range(0, rows, STEP)]
+    pieces += [(r, STEP) for r in range(0, rows - STEP, STEP)]
+    pieces += [(rows - STEP, STEP - 2 * EARLY), (rows - 2 * EARLY, EARLY)]
 
     def send_query(p):
         start, count = pieces[p]
@@ -137,7 +137,7 @@
             copy.start()
         return copies
 
-    query = [send_query(p) for p in range(AHEAD - 1)]
+    query = [send_query(p) for p in range(2)]
 
     @pl.when(jnp.logical_not(last))
     def _():
@@ -176,7 +176,7 @@
     for copy in base:
         copy.start()
     handed = [hand_on(me_q, 0)]
-    query.append(send_query(AHEAD - 1))
+    query += [send_query(p) for p in range(2, len(pieces))]
     turn(me_q)
     for d in range(1, nq // 2):
         base[d - 1].wait_recv()
@@ -298,10 +298,6 @@
     for p in range(1, len(pieces)):
         for copy in query[p]:
             copy.wait_recv()
-        if p + AHEAD - 1 < len(pieces):
-            for copy in query[p]:
-                copy.wait_send()
-            query.append(send_query(p + AHEAD - 1))
         normalize(*pieces[p])
         if p == 1:
 
@@ -309,7 +305,9 @@
             def _():
                 up.wait_recv()
 
-        score(pieces[p][0])
+        if p < len(pieces) - 2:
+            score(pieces[p][0])
+    score(rows - STEP)
 
     peaks = [
         remote(tops.at[0], tops.at[1 + d], top_send.at[d], top_recv.at[d], me_q, z)
@@ -332,8 +330,8 @@
 
     for copy in base + handed:
         copy.wait_send()
-    for p in [0] + list(range(max(1, len(pieces) - AHEAD + 1), len(pieces))):
-        for copy in query[p]:
+    for copies in query:
+        for copy in copies:
             copy.wait_send()
     for copy in written + peaks:
         copy.wait()
@@ -379,8 +377,8 @@
                 dma((nq // 2 - 1,)),
                 dma((nq // 2,)),
                 dma((nq // 2,)),
-                dma((steps + 1, nz - 1)),
-                dma((steps + 1, nz - 1)),
+                dma((steps + 2, nz - 1)),
+                dma((steps + 2, nz - 1)),
                 dma(()),
                 dma(()),
                 dma((nz - 1,)),

time: 40.2 us -> 40.7 us (1.012)
  Pallas kernels: 37.1 us -> 37.7 us
    pallas_call x1, Pallas kernels: 37.1 us -> 37.7 us  [local(): pl.pallas_call(functools.partial(kernel, nq, nz), out_shape=(jax.ShapeDty...]
where the time goes in v6:
time: 40.7 us; the launch traced here: 40.6 us
  Pallas kernels  37.7 us (93%)
  local copies, waits for them, and re-layouts  2.25 us (6%)
  between operations  0.65 us (2%)
    pallas_call x1, Pallas kernels, local(): pl.pallas_call(functools.partial(kernel, nq, nz), out_shape=(jax.ShapeDty...  37.7 us
    unnamed x4, local copies, waits for them, and re-layouts  2.25 us

profile of v6, /device:TPU:0, one launch (start us, length us, event | category | flops | bytes accessed | tf_op | source)
XLA Modules:
  0.0 40.6 jit_solution(8579001595832406799)
XLA Ops:
  0.6 37.7 %shard_map.50 = (bf16[512,256]{1,0:T(8,128)(2,1)}, f32[4,128]{1,0:T(4,128)}) custom-call(bf16[512,256]{1,0:T(8,128)(2,1)} %q_ref.1, bf16[256,128]{1,0:T(8,128)(2,1)} %b_ref.1, s32[5]{0:T(128)} %slopes_hbm.1), custom_call_target="tpu_custom_call" | custom-call | flops 402653184 | bytes 524288 | tf_op jit(solution)/shard_map/pallas_call | solution.py:356
  38.3 0.0 copy-start
  38.3 1.7 %copy.7 = bf16[512,256]{1,0:T(8,128)(2,1)} copy(bf16[512,256]{1,0:T(8,128)(2,1)} %get-tuple-element.8) | data formatting | bytes 524288
  40.0 0.0 copy-done
  40.0 0.6 %copy.8 = f32[512]{0:T(512)} copy(f32[512]{0:T(512)S(1)} %bitcast.1) | data formatting | bytes 4096
Async XLA Ops:
  38.3 1.7 %copy-start = (f32[4,128]{1,0:T(4,128)S(1)}, f32[4,128]{1,0:T(4,128)}, u32[]{:S(2)}) copy-start(f32[4,128]{1,0:T(4,128)} %get-tuple-element.5) | copy-start | bytes 6148
